TPU v7x, 32 devices: a whole 2x2x4 slice. The times are simulated.
32 devices in a mesh: vox: 8 (over y, x, core), frm: 4 (over z).
Axes of the slice: x: 2, y: 2, z: 4, core: 2. Of those that a mesh axis runs over, the one named last changes fastest.
Arguments:
- volume: bfloat16 [512, 32, 128], P('vox', 'frm'), parts along dimension 1, may hold values from 0.099609375 to 2
- measured: bfloat16 [512, 32, 128], P('vox', 'frm'), parts along dimension 1, may hold values from 0.19921875 to 3
- background: float32 [32], P('frm'), parts along dimension 0, may hold values from 0.05 to 0.5
- psf_tiles: bfloat16 [12, 128, 128], replicated, may hold values from 0 to 0.0025939941
- pair_sensor: int32 [8, 12, 64], P('vox'), may hold values from 0 to 63, as said below
- pair_voxel: int32 [8, 12, 64], P('vox'), may hold values from 0 to 511, as said below
- pair_count: int32 [8, 12], P('vox'), may hold values from 1 to 64, as said below
Outputs:
- updated: float32 [512, 32, 128], P('vox', 'frm'), parts along dimension 1
There are 4 independent parts, one for each index of `frm`. A program takes and returns all parts, laid end to end along the dimension named above; an argument that names none is the same for every part. Nothing has to cross between parts.
Inputs may be any that keep to these rules, and one draw needn't show every extreme that they name: `pair_sensor`: the local index of a pair's sensor block among the 64 blocks of the list's own device; within one device's list for one offset all 64 slots name different sensor blocks. `pair_voxel`: a pair in device i's lists names a voxel block held by a device at most 3 positions from i along vox, inside the grid; within one device's list for one offset all 64 slots name different voxel blocks; the list of offset 0 names each of device i's own voxel blocks exactly once. `pair_count`: the live slots of a list are its first ones; every list of offset 0 is full, and for every offset some device's list is full.
All inputs are finite; a program needn't handle non-finite values.
Results may differ from a plain program's by a relative error of at most 0.0003.
Values may be sent and summed in bfloat16 or wider, within the bound.
A program may use at most 64 MiB of HBM per device.

v0:
```python
import jax
import jax.numpy as jnp
from jax import lax
from jax.sharding import PartitionSpec as P

REACH = 3


def passed_along(value, axis, steps):
    count = lax.axis_size(axis)
    initial, last = (max(0, -steps), min(count, count - steps))
    return lax.ppermute(value, axis, [(source, source + steps) for source in range(initial, last)])


def project_forward(window, psf_tiles, take_all, sensor_all, live_counts, blocks):
    frames = window.shape[1]
    slot_count = take_all.shape[1]
    slot_iota = jnp.arange(slot_count, dtype=jnp.int32)
    block_iota = jnp.arange(blocks, dtype=jnp.int32)

    def project_per_offset(offset, totals):
        psf_tile = psf_tiles[offset]
        take_row = lax.dynamic_index_in_dim(take_all, offset, 0, keepdims=False)
        sensor_row = lax.dynamic_index_in_dim(sensor_all, offset, 0, keepdims=False)
        live = slot_iota < live_counts[offset]
        gathered = jnp.take(window, take_row, axis=0).reshape(slot_count, frames * 128)
        placing = ((sensor_row[None, :] == block_iota[:, None]) & live[None, :]).astype(
            jnp.bfloat16
        )
        placed = jnp.dot(placing, gathered, preferred_element_type=jnp.float32).astype(jnp.bfloat16)
        product = jnp.dot(
            placed.reshape(blocks * frames, 128), psf_tile, preferred_element_type=jnp.float32
        )
        return totals + product.reshape(blocks, frames, 128)

    empty_sum = jnp.zeros((blocks, frames, 128), jnp.float32)
    return lax.fori_loop(0, psf_tiles.shape[0], project_per_offset, empty_sum)


def push_backward(extended, psf_tiles, sensor_all, take_all, live_counts, window_rows):
    frames = extended.shape[1]
    slot_count = take_all.shape[1]
    slot_iota = jnp.arange(slot_count, dtype=jnp.int32)
    row_iota = jnp.arange(window_rows, dtype=jnp.int32)

    def push_per_offset(offset, totals):
        psf_tile = psf_tiles[offset]
        take_row = lax.dynamic_index_in_dim(take_all, offset, 0, keepdims=False)
        sensor_row = lax.dynamic_index_in_dim(sensor_all, offset, 0, keepdims=False)
        live = slot_iota < live_counts[offset]
        gathered = jnp.take(extended, sensor_row, axis=0).reshape(slot_count, frames * 128)
        placing = ((take_row[None, :] == row_iota[:, None]) & live[None, :]).astype(jnp.bfloat16)
        placed = jnp.dot(placing, gathered, preferred_element_type=jnp.float32).astype(jnp.bfloat16)
        product = lax.dot_general(
            placed.reshape(window_rows * frames, 128),
            psf_tile,
            (((1,), (1,)), ((), ())),
            preferred_element_type=jnp.float32,
        )
        return totals + product.reshape(window_rows, frames, 128)

    empty_sum = jnp.zeros((window_rows, frames, 128), jnp.float32)
    return lax.fori_loop(0, psf_tiles.shape[0], push_per_offset, empty_sum)


def local(volume, measured, background, psf_tiles, pair_sensor, pair_voxel, pair_count):
    blocks = volume.shape[0]
    frames = volume.shape[1]
    my_index = lax.axis_index("vox")
    sensor_lists = pair_sensor[0]
    voxel_lists = pair_voxel[0]
    live_counts = pair_count[0]
    panels = []
    for shift_by in range(REACH, -REACH - 1, -1):
        if shift_by == 0:
            panels.append(volume)
        else:
            panels.append(passed_along(volume, "vox", shift_by))
    window = jnp.concatenate(panels, axis=0)
    window_base = (my_index - REACH) * blocks
    take_ids = voxel_lists - window_base
    projected = project_forward(window, psf_tiles, take_ids, sensor_lists, live_counts, blocks)
    ratio_image = (measured.astype(jnp.float32) / (projected + background[None, :, None])).astype(
        jnp.bfloat16
    )
    extended = jnp.concatenate([ratio_image, jnp.ones((blocks, 1, 128), jnp.bfloat16)], axis=1)
    partial_value = push_backward(
        extended, psf_tiles, sensor_lists, take_ids, live_counts, (2 * REACH + 1) * blocks
    )
    backproj = partial_value[REACH * blocks : (REACH + 1) * blocks]
    for slab_index in range(2 * REACH + 1):
        if slab_index != REACH:
            slab = partial_value[slab_index * blocks : (slab_index + 1) * blocks]
            backproj = backproj + passed_along(slab, "vox", slab_index - REACH)
    return volume.astype(jnp.float32) * backproj[:, :frames] / backproj[:, frames:]


def solution(mesh):
    return jax.shard_map(
        local,
        mesh=mesh,
        in_specs=(
            P("vox", "frm", None),
            P("vox", "frm", None),
            P("frm"),
            P(),
            P("vox", None, None),
            P("vox", None, None),
            P("vox", None),
        ),
        out_specs=P("vox", "frm", None),
        check_vma=False,
    )
```

profile of v0, /device:TPU:0, one launch (start us, length us, event | category | flops | bytes accessed | tf_op | source)
XLA Modules:
  0.0 211.3 jit_solution(17878504403484223715)
XLA Ops:
  0.0 1.3 collective-permute-start.4
  1.3 1.3 collective-permute-start.3
  2.6 3.0 %collective-permute-start.2 = (bf16[64,8,128]{2,1,0:T(8,128)(2,1)}, bf16[64,8,128]{2,1,0:T(8,128)(2,1)S(1)}, u32[]{:S(2)}, u32[]{:S(2)}) collective-permute-start(bf16[64,8,128]{2,1,0:T(8,128)(2,1)} %param.11), channel_id=1, source_target_pairs={{0,4},{4,8},{8,12},{12,16},{16,20},{20,24},{24,28},{1,5},{5,9},{9,... | collective-permute-start | bytes 393224 | tf_op jit(solution)/shard_map/ppermute | solution.py:12
  5.6 5.5 %collective-permute-start.1 = (bf16[64,8,128]{2,1,0:T(8,128)(2,1)}, bf16[64,8,128]{2,1,0:T(8,128)(2,1)S(1)}, u32[]{:S(2)}, u32[]{:S(2)}) collective-permute-start(bf16[64,8,128]{2,1,0:T(8,128)(2,1)} %param.11), channel_id=1, source_target_pairs={{0,8},{4,12},{8,16},{12,20},{16,24},{20,28},{1,9},{5,13},{9,17},{1... | collective-permute-start | bytes 393224 | tf_op jit(solution)/shard_map/ppermute | solution.py:12
  11.1 4.9 %collective-permute-start = (bf16[64,8,128]{2,1,0:T(8,128)(2,1)}, bf16[64,8,128]{2,1,0:T(8,128)(2,1)S(1)}, u32[]{:S(2)}, u32[]{:S(2)}) collective-permute-start(bf16[64,8,128]{2,1,0:T(8,128)(2,1)} %param.11), channel_id=1, source_target_pairs={{0,12},{4,16},{8,20},{12,24},{16,28},{1,13},{5,17},{9,21},{13,25},... | collective-permute-start | bytes 393224 | tf_op jit(solution)/shard_map/ppermute | solution.py:12
  16.8 2.1 collective-permute-done
  18.9 1.3 collective-permute-start.5
  21.3 4.1 %collective-permute-done.5 = bf16[64,8,128]{2,1,0:T(8,128)(2,1)S(1)} collective-permute-done((bf16[64,8,128]{2,1,0:T(8,128)(2,1)}, bf16[64,8,128]{2,1,0:T(8,128)(2,1)S(1)}, u32[]{:S(2)}, u32[]{:S(2)}) %collective-permute-start.5) | collective-permute-done | bytes 131104 | tf_op jit(solution)/shard_map/ppermute | solution.py:12
  25.5 44.9 %while.31 = (s32[]{:T(128)}, f32[64,8,128]{2,1,0:T(8,128)S(1)}, s32[12,64]{1,0:T(8,128)S(1)}, s32[12]{0:T(128)}, s32[12,64]{1,0:T(8,128)S(1)}, /*index=5*/bf16[4...) while((s32[]{:T(128)}, f32[64,8,128]{2,1,0:T(8,128)S(1)}, ...), condition=%wide.region_1.2_spmd.clone.clone, body=%wide.region_0.1_spmd.clone.clone.sunk | while | flops 25437828 | bytes 1481103 | solution.py:37
  25.5 1.3 dynamic_slice.116
  70.6 86.0 %while.30 = (s32[]{:T(128)}, f32[448,9,128]{2,0,1:T(8,128)}, s32[12,64]{1,0:T(8,128)S(1)}, s32[12]{0:T(128)}, s32[12,64]{1,0:T(8,128)S(1)}, /*index=5*/bf16[64,9...) while((s32[]{:T(128)}, f32[448,9,128]{2,0,1:T(8,128)}, ...), condition=%wide.region_3.4_spmd.clone, body=%wide.region_2.3_spmd.clone.sunk | while | flops 199861888 | bytes 8739215 | solution.py:63
  74.4 2.6 %select_add_fusion.2 = f32[448,9,128]{2,0,1:T(8,128)} fusion(f32[448,9,128]{2,0,1:T(8,128)} %get-tuple-element.572, bf16[448,9,128]{0,2,1:T(8,128)(2,1)S(1)} %bitcast.88, pred[]{:T(512)S(6)} %compare.7, bf16[12,128,128]{2,1,0:T(8,128)(2,1)} %get-tuple-element.586, s32[]{:T(128)S(6)} %copy.66), kind=kOutput, calls=%fused_computation.6.clone.1 | convolution fusion | flops 133152768 | bytes 5193733 | tf_op jit(solution)/shard_map/while/body/eval_jaxpr/dot_general | solution.py:54
  80.8 3.4 %select_add_fusion.2 = f32[448,9,128]{2,0,1:T(8,128)} fusion(f32[448,9,128]{2,0,1:T(8,128)} %get-tuple-element.572, bf16[448,9,128]{0,2,1:T(8,128)(2,1)S(1)} %bitcast.88, pred[]{:T(512)S(6)} %compare.7, bf16[12,128,128]{2,1,0:T(8,128)(2,1)} %get-tuple-element.586, s32[]{:T(128)S(6)} %copy.66), kind=kOutput, calls=%fused_computation.6.clone.1 | convolution fusion | flops 133152768 | bytes 5193733 | tf_op jit(solution)/shard_map/while/body/eval_jaxpr/dot_general | solution.py:54
  88.0 3.4 %select_add_fusion.2 = f32[448,9,128]{2,0,1:T(8,128)} fusion(f32[448,9,128]{2,0,1:T(8,128)} %get-tuple-element.572, bf16[448,9,128]{0,2,1:T(8,128)(2,1)S(1)} %bitcast.88, pred[]{:T(512)S(6)} %compare.7, bf16[12,128,128]{2,1,0:T(8,128)(2,1)} %get-tuple-element.586, s32[]{:T(128)S(6)} %copy.66), kind=kOutput, calls=%fused_computation.6.clone.1 | convolution fusion | flops 133152768 | bytes 5193733 | tf_op jit(solution)/shard_map/while/body/eval_jaxpr/dot_general | solution.py:54
  95.2 3.4 %select_add_fusion.2 = f32[448,9,128]{2,0,1:T(8,128)} fusion(f32[448,9,128]{2,0,1:T(8,128)} %get-tuple-element.572, bf16[448,9,128]{0,2,1:T(8,128)(2,1)S(1)} %bitcast.88, pred[]{:T(512)S(6)} %compare.7, bf16[12,128,128]{2,1,0:T(8,128)(2,1)} %get-tuple-element.586, s32[]{:T(128)S(6)} %copy.66), kind=kOutput, calls=%fused_computation.6.clone.1 | convolution fusion | flops 133152768 | bytes 5193733 | tf_op jit(solution)/shard_map/while/body/eval_jaxpr/dot_general | solution.py:54
  102.5 3.4 %select_add_fusion.2 = f32[448,9,128]{2,0,1:T(8,128)} fusion(f32[448,9,128]{2,0,1:T(8,128)} %get-tuple-element.572, bf16[448,9,128]{0,2,1:T(8,128)(2,1)S(1)} %bitcast.88, pred[]{:T(512)S(6)} %compare.7, bf16[12,128,128]{2,1,0:T(8,128)(2,1)} %get-tuple-element.586, s32[]{:T(128)S(6)} %copy.66), kind=kOutput, calls=%fused_computation.6.clone.1 | convolution fusion | flops 133152768 | bytes 5193733 | tf_op jit(solution)/shard_map/while/body/eval_jaxpr/dot_general | solution.py:54
  109.7 3.4 %select_add_fusion.2 = f32[448,9,128]{2,0,1:T(8,128)} fusion(f32[448,9,128]{2,0,1:T(8,128)} %get-tuple-element.572, bf16[448,9,128]{0,2,1:T(8,128)(2,1)S(1)} %bitcast.88, pred[]{:T(512)S(6)} %compare.7, bf16[12,128,128]{2,1,0:T(8,128)(2,1)} %get-tuple-element.586, s32[]{:T(128)S(6)} %copy.66), kind=kOutput, calls=%fused_computation.6.clone.1 | convolution fusion | flops 133152768 | bytes 5193733 | tf_op jit(solution)/shard_map/while/body/eval_jaxpr/dot_general | solution.py:54
  116.9 3.4 %select_add_fusion.2 = f32[448,9,128]{2,0,1:T(8,128)} fusion(f32[448,9,128]{2,0,1:T(8,128)} %get-tuple-element.572, bf16[448,9,128]{0,2,1:T(8,128)(2,1)S(1)} %bitcast.88, pred[]{:T(512)S(6)} %compare.7, bf16[12,128,128]{2,1,0:T(8,128)(2,1)} %get-tuple-element.586, s32[]{:T(128)S(6)} %copy.66), kind=kOutput, calls=%fused_computation.6.clone.1 | convolution fusion | flops 133152768 | bytes 5193733 | tf_op jit(solution)/shard_map/while/body/eval_jaxpr/dot_general | solution.py:54
  124.2 3.4 %select_add_fusion.2 = f32[448,9,128]{2,0,1:T(8,128)} fusion(f32[448,9,128]{2,0,1:T(8,128)} %get-tuple-element.572, bf16[448,9,128]{0,2,1:T(8,128)(2,1)S(1)} %bitcast.88, pred[]{:T(512)S(6)} %compare.7, bf16[12,128,128]{2,1,0:T(8,128)(2,1)} %get-tuple-element.586, s32[]{:T(128)S(6)} %copy.66), kind=kOutput, calls=%fused_computation.6.clone.1 | convolution fusion | flops 133152768 | bytes 5193733 | tf_op jit(solution)/shard_map/while/body/eval_jaxpr/dot_general | solution.py:54
  131.4 3.4 %select_add_fusion.2 = f32[448,9,128]{2,0,1:T(8,128)} fusion(f32[448,9,128]{2,0,1:T(8,128)} %get-tuple-element.572, bf16[448,9,128]{0,2,1:T(8,128)(2,1)S(1)} %bitcast.88, pred[]{:T(512)S(6)} %compare.7, bf16[12,128,128]{2,1,0:T(8,128)(2,1)} %get-tuple-element.586, s32[]{:T(128)S(6)} %copy.66), kind=kOutput, calls=%fused_computation.6.clone.1 | convolution fusion | flops 133152768 | bytes 5193733 | tf_op jit(solution)/shard_map/while/body/eval_jaxpr/dot_general | solution.py:54
  138.6 3.4 %select_add_fusion.2 = f32[448,9,128]{2,0,1:T(8,128)} fusion(f32[448,9,128]{2,0,1:T(8,128)} %get-tuple-element.572, bf16[448,9,128]{0,2,1:T(8,128)(2,1)S(1)} %bitcast.88, pred[]{:T(512)S(6)} %compare.7, bf16[12,128,128]{2,1,0:T(8,128)(2,1)} %get-tuple-element.586, s32[]{:T(128)S(6)} %copy.66), kind=kOutput, calls=%fused_computation.6.clone.1 | convolution fusion | flops 133152768 | bytes 5193733 | tf_op jit(solution)/shard_map/while/body/eval_jaxpr/dot_general | solution.py:54
  145.9 3.4 %select_add_fusion.2 = f32[448,9,128]{2,0,1:T(8,128)} fusion(f32[448,9,128]{2,0,1:T(8,128)} %get-tuple-element.572, bf16[448,9,128]{0,2,1:T(8,128)(2,1)S(1)} %bitcast.88, pred[]{:T(512)S(6)} %compare.7, bf16[12,128,128]{2,1,0:T(8,128)(2,1)} %get-tuple-element.586, s32[]{:T(128)S(6)} %copy.66), kind=kOutput, calls=%fused_computation.6.clone.1 | convolution fusion | flops 133152768 | bytes 5193733 | tf_op jit(solution)/shard_map/while/body/eval_jaxpr/dot_general | solution.py:54
  153.1 3.4 %select_add_fusion.2 = f32[448,9,128]{2,0,1:T(8,128)} fusion(f32[448,9,128]{2,0,1:T(8,128)} %get-tuple-element.572, bf16[448,9,128]{0,2,1:T(8,128)(2,1)S(1)} %bitcast.88, pred[]{:T(512)S(6)} %compare.7, bf16[12,128,128]{2,1,0:T(8,128)(2,1)} %get-tuple-element.586, s32[]{:T(128)S(6)} %copy.66), kind=kOutput, calls=%fused_computation.6.clone.1 | convolution fusion | flops 133152768 | bytes 5193733 | tf_op jit(solution)/shard_map/while/body/eval_jaxpr/dot_general | solution.py:54
  156.5 2.9 %copy.20 = f32[448,9,128]{2,1,0:T(8,128)S(1)} copy(f32[448,9,128]{2,0,1:T(8,128)} %get-tuple-element.326) | data formatting | bytes 4128768 | tf_op jit(solution)/shard_map/while | solution.py:63
  159.8 1.3 collective-permute-start.6
  161.1 4.9 %collective-permute-start.11 = (f32[64,9,128]{2,1,0:T(8,128)S(1)}, f32[64,9,128]{2,1,0:T(8,128)S(1)}, u32[]{:S(2)}, u32[]{:S(2)}) collective-permute-start(f32[64,9,128]{2,1,0:T(8,128)S(1)} %get-tuple-element.434), channel_id=1, source_target_pairs={{0,12},{4,16},{8,20},{12,24},{16,28},{1,13},{5,17},{9,21},{13,25},... | collective-permute-start | bytes 884744 | tf_op jit(solution)/shard_map/ppermute | solution.py:12
  166.0 3.8 %collective-permute-start.10 = (f32[64,9,128]{2,1,0:T(8,128)S(1)}, f32[64,9,128]{2,1,0:T(8,128)S(1)}, u32[]{:S(2)}, u32[]{:S(2)}) collective-permute-start(f32[64,9,128]{2,1,0:T(8,128)S(1)} %get-tuple-element.435), channel_id=1, source_target_pairs={{0,8},{4,12},{8,16},{12,20},{16,24},{20,28},{1,9},{5,13},{9,17},{1... | collective-permute-start | bytes 884744 | tf_op jit(solution)/shard_map/ppermute | solution.py:12
  169.8 1.9 collective-permute-start.9
  171.7 1.3 collective-permute-start.8
  173.0 1.4 collective-permute-start.7
  175.1 11.2 %collective-permute-done.10 = f32[64,9,128]{2,1,0:T(8,128)S(1)} collective-permute-done((f32[64,9,128]{2,1,0:T(8,128)S(1)}, f32[64,9,128]{2,1,0:T(8,128)S(1)}, u32[]{:S(2)}, u32[]{:S(2)}) %collective-permute-start.10) | collective-permute-done | bytes 294944 | tf_op jit(solution)/shard_map/ppermute | solution.py:12
  186.3 23.9 %collective-permute-done.7 = f32[64,9,128]{2,1,0:T(8,128)S(1)} collective-permute-done((f32[64,9,128]{2,1,0:T(8,128)S(1)}, f32[64,9,128]{2,1,0:T(8,128)S(1)}, u32[]{:S(2)}, u32[]{:S(2)}) %collective-permute-start.7) | collective-permute-done | bytes 294944 | tf_op jit(solution)/shard_map/ppermute | solution.py:12
  (233 shorter events, 91.9 us)
Async XLA Ops:
  0.0 21.2 %collective-permute-start.4 = (bf16[64,8,128]{2,1,0:T(8,128)(2,1)}, bf16[64,8,128]{2,1,0:T(8,128)(2,1)S(1)}, u32[]{:S(2)}, u32[]{:S(2)}) collective-permute-start(bf16[64,8,128]{2,1,0:T(8,128)(2,1)} %param.11), channel_id=1, source_target_pairs={{8,0},{12,4},{16,8},{20,12},{24,16},{28,20},{9,1},{13,5},{17,9},{2... | collective-permute-start | bytes 393224 | tf_op jit(solution)/shard_map/ppermute | solution.py:12
  1.3 19.9 %collective-permute-start.3 = (bf16[64,8,128]{2,1,0:T(8,128)(2,1)}, bf16[64,8,128]{2,1,0:T(8,128)(2,1)S(1)}, u32[]{:S(2)}, u32[]{:S(2)}) collective-permute-start(bf16[64,8,128]{2,1,0:T(8,128)(2,1)} %param.11), channel_id=1, source_target_pairs={{4,0},{8,4},{12,8},{16,12},{20,16},{24,20},{28,24},{5,1},{9,5},{13... | collective-permute-start | bytes 393224 | tf_op jit(solution)/shard_map/ppermute | solution.py:12
  2.6 17.6 %collective-permute-start.2 = (bf16[64,8,128]{2,1,0:T(8,128)(2,1)}, bf16[64,8,128]{2,1,0:T(8,128)(2,1)S(1)}, u32[]{:S(2)}, u32[]{:S(2)}) collective-permute-start(bf16[64,8,128]{2,1,0:T(8,128)(2,1)} %param.11), channel_id=1, source_target_pairs={{0,4},{4,8},{8,12},{12,16},{16,20},{20,24},{24,28},{1,5},{5,9},{9,... | collective-permute-start | bytes 393224 | tf_op jit(solution)/shard_map/ppermute | solution.py:12
  5.6 14.6 %collective-permute-start.1 = (bf16[64,8,128]{2,1,0:T(8,128)(2,1)}, bf16[64,8,128]{2,1,0:T(8,128)(2,1)S(1)}, u32[]{:S(2)}, u32[]{:S(2)}) collective-permute-start(bf16[64,8,128]{2,1,0:T(8,128)(2,1)} %param.11), channel_id=1, source_target_pairs={{0,8},{4,12},{8,16},{12,20},{16,24},{20,28},{1,9},{5,13},{9,17},{1... | collective-permute-start | bytes 393224 | tf_op jit(solution)/shard_map/ppermute | solution.py:12
  11.1 7.8 %collective-permute-start = (bf16[64,8,128]{2,1,0:T(8,128)(2,1)}, bf16[64,8,128]{2,1,0:T(8,128)(2,1)S(1)}, u32[]{:S(2)}, u32[]{:S(2)}) collective-permute-start(bf16[64,8,128]{2,1,0:T(8,128)(2,1)} %param.11), channel_id=1, source_target_pairs={{0,12},{4,16},{8,20},{12,24},{16,28},{1,13},{5,17},{9,21},{13,25},... | collective-permute-start | bytes 393224 | tf_op jit(solution)/shard_map/ppermute | solution.py:12
  18.9 6.5 %collective-permute-start.5 = (bf16[64,8,128]{2,1,0:T(8,128)(2,1)}, bf16[64,8,128]{2,1,0:T(8,128)(2,1)S(1)}, u32[]{:S(2)}, u32[]{:S(2)}) collective-permute-start(bf16[64,8,128]{2,1,0:T(8,128)(2,1)} %param.11), channel_id=1, source_target_pairs={{12,0},{16,4},{20,8},{24,12},{28,16},{13,1},{17,5},{21,9},{25,13},... | collective-permute-start | bytes 393224 | tf_op jit(solution)/shard_map/ppermute | solution.py:12
  25.4 45.0 %copy-start.1 = (bf16[64,8,128]{2,1,0:T(8,128)(2,1)S(1)}, bf16[64,8,128]{2,1,0:T(8,128)(2,1)}, u32[]{:S(2)}) copy-start(bf16[64,8,128]{2,1,0:T(8,128)(2,1)} %param.12) | copy-start | bytes 393220
  25.4 45.0 %copy-start.2 = (f32[8]{0:T(128)S(1)}, f32[8]{0:T(128)}, u32[]{:S(2)}) copy-start(f32[8]{0:T(128)} %param.13) | copy-start | bytes 100
  159.8 13.2 %collective-permute-start.6 = (f32[64,9,128]{2,1,0:T(8,128)S(1)}, f32[64,9,128]{2,1,0:T(8,128)S(1)}, u32[]{:S(2)}, u32[]{:S(2)}) collective-permute-start(f32[64,9,128]{2,1,0:T(8,128)S(1)} %get-tuple-element.433), channel_id=1, source_target_pairs={{12,0},{16,4},{20,8},{24,12},{28,16},{13,1},{17,5},{21,9},{25,13},... | collective-permute-start | bytes 884744 | tf_op jit(solution)/shard_map/ppermute | solution.py:12
  161.1 14.0 %collective-permute-start.11 = (f32[64,9,128]{2,1,0:T(8,128)S(1)}, f32[64,9,128]{2,1,0:T(8,128)S(1)}, u32[]{:S(2)}, u32[]{:S(2)}) collective-permute-start(f32[64,9,128]{2,1,0:T(8,128)S(1)} %get-tuple-element.434), channel_id=1, source_target_pairs={{0,12},{4,16},{8,20},{12,24},{16,28},{1,13},{5,17},{9,21},{13,25},... | collective-permute-start | bytes 884744 | tf_op jit(solution)/shard_map/ppermute | solution.py:12
  166.0 20.3 %collective-permute-start.10 = (f32[64,9,128]{2,1,0:T(8,128)S(1)}, f32[64,9,128]{2,1,0:T(8,128)S(1)}, u32[]{:S(2)}, u32[]{:S(2)}) collective-permute-start(f32[64,9,128]{2,1,0:T(8,128)S(1)} %get-tuple-element.435), channel_id=1, source_target_pairs={{0,8},{4,12},{8,16},{12,20},{16,24},{20,28},{1,9},{5,13},{9,17},{1... | collective-permute-start | bytes 884744 | tf_op jit(solution)/shard_map/ppermute | solution.py:12
  169.8 16.5 %collective-permute-start.9 = (f32[64,9,128]{2,1,0:T(8,128)S(1)}, f32[64,9,128]{2,1,0:T(8,128)S(1)}, u32[]{:S(2)}, u32[]{:S(2)}) collective-permute-start(f32[64,9,128]{2,1,0:T(8,128)S(1)} %get-tuple-element.436), channel_id=1, source_target_pairs={{0,4},{4,8},{8,12},{12,16},{16,20},{20,24},{24,28},{1,5},{5,9},{9,... | collective-permute-start | bytes 884744 | tf_op jit(solution)/shard_map/ppermute | solution.py:12
  171.7 14.6 %collective-permute-start.8 = (f32[64,9,128]{2,1,0:T(8,128)S(1)}, f32[64,9,128]{2,1,0:T(8,128)S(1)}, u32[]{:S(2)}, u32[]{:S(2)}) collective-permute-start(f32[64,9,128]{2,1,0:T(8,128)S(1)} %get-tuple-element.437), channel_id=1, source_target_pairs={{4,0},{8,4},{12,8},{16,12},{20,16},{24,20},{28,24},{5,1},{9,5},{13... | collective-permute-start | bytes 884744 | tf_op jit(solution)/shard_map/ppermute | solution.py:12
  173.0 37.5 %copy-start = (bf16[64,8,128]{2,1,0:T(8,128)(2,1)S(1)}, bf16[64,8,128]{2,1,0:T(8,128)(2,1)}, u32[]{:S(2)}) copy-start(bf16[64,8,128]{2,1,0:T(8,128)(2,1)} %param.11) | copy-start | bytes 393220
  173.0 37.2 %collective-permute-start.7 = (f32[64,9,128]{2,1,0:T(8,128)S(1)}, f32[64,9,128]{2,1,0:T(8,128)S(1)}, u32[]{:S(2)}, u32[]{:S(2)}) collective-permute-start(f32[64,9,128]{2,1,0:T(8,128)S(1)} %get-tuple-element.438), channel_id=1, source_target_pairs={{8,0},{12,4},{16,8},{20,12},{24,16},{28,20},{9,1},{13,5},{17,9},{2... | collective-permute-start | bytes 884744 | tf_op jit(solution)/shard_map/ppermute | solution.py:12
where the time goes:
time: 213 us; the launch traced here: 211 us
  matrix products  60.8 us (29%)
  local copies, waits for them, and re-layouts  59.2 us (28%)
  waiting for transfers between devices  42 us (20%)
  starting transfers between devices  31.9 us (15%)
  other arithmetic  15.9 us (7%)
    ppermute x12, waiting for transfers between devices, passed_along(): lax.ppermute(value, axis, [(source, source + steps) for source in range(i...  42 us
    dot_general x12, matrix products, push_per_offset(): lax.dot_general(placed.reshape(window_rows * frames, 128), psf_tile, (((1...  40.5 us
    ppermute x12, starting transfers between devices, passed_along(): lax.ppermute(value, axis, [(source, source + steps) for source in range(i...  31.9 us
    dynamic_slice x12, local copies, waits for them, and re-layouts, project_per_offset(): live = slot_iota < live_counts[offset]  14.9 us
    dynamic_slice x12, local copies, waits for them, and re-layouts, push_per_offset(): live = slot_iota < live_counts[offset]  14.8 us
    dot_general x12, matrix products, project_per_offset(): jnp.dot(placed.reshape(blocks * frames, 128), psf_tile, preferred_element...  11.6 us
    convert_element_type x12, local copies, waits for them, and re-layouts, push_per_offset(): jnp.dot(placing, gathered, preferred_element_type=jnp.float32)  9.67 us
    gather x12, local copies, waits for them, and re-layouts, push_per_offset(): jnp.take(extended, sensor_row, axis=0).reshape(slot_count, frames * 128)  7.59 us
  transfers between devices with their start and end apart: 12, of which 5 were waited for; matrix products, arithmetic and copies ran while one was open for 1% of the time, Pallas kernels for 0%

commit v1 on v0

v1 whole, which is shorter than its diff:
```python
import functools

import jax
import jax.numpy as jnp
from jax import lax
from jax.experimental import pallas as pl
from jax.experimental.pallas import tpu as pltpu
from jax.sharding import PartitionSpec as P

REACH = 3
PANELS = 2 * REACH + 2
FAR = -1000000.0
SHIFTS = (1, -1, 2, -2, 3, -3)


def update_kernel(
    count,
    chunks,
    volume_ref,
    measured_ref,
    background_ref,
    psf_ref,
    sensor_ref,
    voxel_ref,
    live_ref,
    out_ref,
    volume_win,
    ratio_win,
    voxel_win,
    volume_f32,
    measured_f32,
    place_fwd,
    place_bwd,
    psf_flat,
    psf_turned,
    ones_rows,
    norm,
    send_list,
    recv_list,
    send_vol,
    recv_vol,
    send_ratio,
    recv_ratio,
):
    me = lax.axis_index("vox")
    blocks, frames, width = volume_ref.shape
    offsets = psf_ref.shape[0]
    per = frames // chunks
    lanes = per * width
    f32, bf16 = jnp.float32, jnp.bfloat16

    def inside(shift):
        return (me + shift >= 0) & (me + shift < count)

    barrier = pltpu.get_barrier_semaphore()
    for shift in SHIFTS:

        @pl.when(inside(shift))
        def _():
            pl.semaphore_signal(
                barrier, inc=1, device_id={"vox": me + shift}, device_id_type=pl.DeviceIdType.MESH
            )

    volume_f32[...] = volume_ref[...].astype(f32).reshape(blocks * frames, width)
    for frame in range(frames):
        rows = volume_f32[pl.ds(frame, blocks, stride=frames), :]
        j, k = divmod(frame, per)
        volume_win[j, REACH, :, k * width : (k + 1) * width] = rows.astype(bf16)

    sensor_iota = lax.broadcasted_iota(jnp.int32, (blocks, blocks), 0)
    slot_iota = lax.broadcasted_iota(jnp.int32, (1, blocks), 1)
    lane_iota = lax.broadcasted_iota(jnp.int32, (blocks, 128), 1)
    by_sensor = []
    table = jnp.full((blocks, 128), FAR, f32)
    for o in range(offsets):
        live = slot_iota < live_ref[0, o]
        sensor_row = jnp.where(live, sensor_ref[0, o : o + 1, :], -1)
        voxel_row = voxel_ref[0, o : o + 1, :].astype(f32) - FAR
        column = jnp.sum(
            jnp.where(sensor_row == sensor_iota, voxel_row, 0.0), axis=1, keepdims=True
        ) + FAR
        by_sensor.append(column)
        table = jnp.where(lane_iota == o, column, table)
    voxel_win[REACH, :, :blocks] = table.T[:16, :]
    voxel_win[REACH, :, blocks:] = jnp.full((16, 128 - blocks), FAR, f32)

    pl.semaphore_wait(barrier, jnp.minimum(me, REACH) + jnp.minimum(count - 1 - me, REACH))

    def remote(buf, index, shift, send_sem, recv_sem):
        return pltpu.make_async_remote_copy(
            src_ref=buf.at[(*index, REACH)],
            dst_ref=buf.at[(*index, REACH - shift)],
            send_sem=send_sem,
            recv_sem=recv_sem,
            device_id={"vox": me + shift},
            device_id_type=pl.DeviceIdType.MESH,
        )

    def list_copy(i):
        shift = SHIFTS[i]
        return remote(voxel_win, (), shift, send_list.at[i], recv_list.at[i])

    def vol_copy(j, i):
        return remote(volume_win, (j,), SHIFTS[i], send_vol.at[j, i], recv_vol.at[j, i])

    def ratio_copy(j, i):
        return remote(ratio_win, (j,), SHIFTS[i], send_ratio.at[j, i], recv_ratio.at[j, i])

    def each(make, start):
        for i, shift in enumerate(SHIFTS):
            if start:

                @pl.when(inside(shift))
                def _():
                    make(i).start()

            else:

                @pl.when(inside(-shift))
                def _():
                    make(i).wait_recv()

    each(lambda i: vol_copy(0, i), True)
    each(list_copy, True)
    for j in range(1, chunks):
        each(functools.partial(vol_copy, j), True)

    for j in range(chunks):
        volume_win[j, PANELS - 1] = jnp.zeros((blocks, lanes), bf16)
        ratio_win[j, PANELS - 1] = jnp.zeros((blocks, lanes), bf16)
    for shift in SHIFTS:

        @pl.when(jnp.logical_not(inside(shift)))
        def _():
            for j in range(chunks):
                volume_win[j, REACH + shift] = jnp.zeros((blocks, lanes), bf16)
                ratio_win[j, REACH + shift] = jnp.zeros((blocks, lanes), bf16)
            voxel_win[REACH + shift] = jnp.full((16, 128), FAR, f32)

    base = ((me - REACH) * blocks).astype(f32)
    win_iota = lax.broadcasted_iota(jnp.int32, (1, PANELS * blocks), 1).astype(f32) + base
    for o in range(offsets):
        place_fwd[o * blocks : (o + 1) * blocks, :] = jnp.where(
            by_sensor[o] == win_iota, 1.0, 0.0
        ).astype(bf16)
        psf_flat[o * width : (o + 1) * width, :] = psf_ref[o]
        psf_turned[o * width : (o + 1) * width, :] = psf_ref[o].astype(f32).T.astype(bf16)
    measured_f32[...] = measured_ref[...].astype(f32).reshape(blocks * frames, width)

    each(list_copy, False)
    tables = jnp.concatenate(
        [voxel_win[d, :, :blocks] for d in range(PANELS - 1)]
        + [jnp.full((16, blocks), FAR, f32)],
        axis=1,
    )
    voxel_iota = lax.broadcasted_iota(jnp.int32, (blocks, 1), 0).astype(f32) + (
        me * blocks
    ).astype(f32)
    for o in range(offsets):
        hits = jnp.where(tables[o : o + 1, :] == voxel_iota, 1.0, 0.0)
        place_bwd[o * blocks : (o + 1) * blocks, :] = hits.astype(bf16)
        pairs = jnp.sum(hits, axis=1, keepdims=True)
        ones_rows[:, o * width : (o + 1) * width] = jnp.broadcast_to(pairs, (blocks, width)).astype(
            bf16
        )
    norm[...] = jnp.dot(ones_rows[...], psf_turned[...], preferred_element_type=f32)

    def joined(placed):
        return jnp.concatenate(
            [
                jnp.concatenate(
                    [
                        placed[o * blocks : (o + 1) * blocks, k * width : (k + 1) * width]
                        for o in range(offsets)
                    ],
                    axis=1,
                )
                for k in range(per)
            ],
            axis=0,
        )

    for j in range(chunks):
        each(functools.partial(vol_copy, j), False)
        window = volume_win[j].reshape(PANELS * blocks, lanes)
        placed = jnp.dot(place_fwd[...], window, preferred_element_type=f32).astype(bf16)
        projected = jnp.dot(joined(placed), psf_flat[...], preferred_element_type=f32)
        for k in range(per):
            frame = j * per + k
            recorded = measured_f32[pl.ds(frame, blocks, stride=frames), :]
            ratio = recorded / (projected[k * blocks : (k + 1) * blocks] + background_ref[0, frame])
            ratio_win[j, REACH, :, k * width : (k + 1) * width] = ratio.astype(bf16)
        each(functools.partial(ratio_copy, j), True)

    for j in range(chunks):
        each(functools.partial(ratio_copy, j), False)
        window = ratio_win[j].reshape(PANELS * blocks, lanes)
        summed = jnp.dot(place_bwd[...], window, preferred_element_type=f32)
        high = summed.astype(bf16)
        low = (summed - high.astype(f32)).astype(bf16)
        back = jnp.dot(joined(high), psf_turned[...], preferred_element_type=f32)
        back = back + jnp.dot(joined(low), psf_turned[...], preferred_element_type=f32)
        for k in range(per):
            frame = j * per + k
            current = volume_f32[pl.ds(frame, blocks, stride=frames), :]
            out_ref[pl.ds(frame, blocks, stride=frames), :] = (
                current * back[k * blocks : (k + 1) * blocks] / norm[...]
            )

    for i, shift in enumerate(SHIFTS):

        @pl.when(inside(shift))
        def _():
            list_copy(i).wait_send()
            for j in range(chunks):
                vol_copy(j, i).wait_send()
                ratio_copy(j, i).wait_send()


def local(count, volume, measured, background, psf_tiles, pair_sensor, pair_voxel, pair_count):
    blocks, frames, width = volume.shape
    offsets = psf_tiles.shape[0]
    chunks = 4
    lanes = frames // chunks * width
    vmem = pl.BlockSpec(memory_space=pltpu.VMEM)
    smem = pl.BlockSpec(memory_space=pltpu.SMEM)
    links = len(SHIFTS)
    dma = pltpu.SemaphoreType.DMA
    updated = pl.pallas_call(
        functools.partial(update_kernel, count, chunks),
        out_shape=jax.ShapeDtypeStruct((blocks * frames, width), jnp.float32),
        in_specs=[vmem, vmem, smem, vmem, vmem, vmem, smem],
        out_specs=vmem,
        scratch_shapes=[
            pltpu.VMEM((chunks, PANELS, blocks, lanes), jnp.bfloat16),
            pltpu.VMEM((chunks, PANELS, blocks, lanes), jnp.bfloat16),
            pltpu.VMEM((PANELS - 1, 16, 128), jnp.float32),
            pltpu.VMEM((blocks * frames, width), jnp.float32),
            pltpu.VMEM((blocks * frames, width), jnp.float32),
            pltpu.VMEM((offsets * blocks, PANELS * blocks), jnp.bfloat16),
            pltpu.VMEM((offsets * blocks, PANELS * blocks), jnp.bfloat16),
            pltpu.VMEM((offsets * width, width), jnp.bfloat16),
            pltpu.VMEM((offsets * width, width), jnp.bfloat16),
            pltpu.VMEM((blocks, offsets * width), jnp.bfloat16),
            pltpu.VMEM((blocks, width), jnp.float32),
            dma((links,)),
            dma((links,)),
            dma((chunks, links)),
            dma((chunks, links)),
            dma((chunks, links)),
            dma((chunks, links)),
        ],
        compiler_params=pltpu.CompilerParams(
            collective_id=0, has_side_effects=True, vmem_limit_bytes=40 * 1024 * 1024
        ),
    )(
        volume,
        measured,
        background.reshape(1, frames),
        psf_tiles,
        pair_sensor,
        pair_voxel,
        pair_count,
    )
    return updated.reshape(blocks, frames, width)


def solution(mesh):
    return jax.shard_map(
        functools.partial(local, mesh.shape["vox"]),
        mesh=mesh,
        in_specs=(
            P("vox", "frm", None),
            P("vox", "frm", None),
            P("frm"),
            P(),
            P("vox", None, None),
            P("vox", None, None),
            P("vox", None),
        ),
        out_specs=P("vox", "frm", None),
        check_vma=False,
    )
```

time: 213 us -> 35.9 us (0.17)
  matrix products: 60.8 us -> 0 us
  local copies, waits for them, and re-layouts: 59.2 us -> 4.88 us
  waiting for transfers between devices: 42 us -> 0 us
  starting transfers between devices: 31.9 us -> 0 us
  Pallas kernels: 0 us -> 30.8 us
  other arithmetic: 15.9 us -> 0 us
    dot_general x48 -> x0, matrix products: 60.8 us -> none  [the longest x12 40.5 us: push_per_offset(): lax.dot_general(placed.reshape(window_rows * frames, 128), psf_tile, (((1...]
    ppermute x12 -> x0, waiting for transfers between devices: 42 us -> none  [passed_along(): lax.ppermute(value, axis, [(source, source + steps) for source in range(i...]
    ppermute x12 -> x0, starting transfers between devices: 31.9 us -> none  [passed_along(): lax.ppermute(value, axis, [(source, source + steps) for source in range(i...]
    pallas_call x0 -> x1, Pallas kernels: none -> 30.8 us  [local(): pl.pallas_call(functools.partial(update_kernel, count, chunks), out_shape...]
    dynamic_slice x24 -> x0, local copies, waits for them, and re-layouts: 29.7 us -> none  [the longest x12 14.9 us: project_per_offset(): live = slot_iota < live_counts[offset]]
    gather x24 -> x0, local copies, waits for them, and re-layouts: 15.2 us -> none  [the longest x12 7.59 us: push_per_offset(): jnp.take(extended, sensor_row, axis=0).reshape(slot_count, frames * 128)]
    and x24 -> x0, other arithmetic: 13.8 us -> none  [the longest x12 6.88 us: project_per_offset(): jnp.take(window, take_row, axis=0).reshape(slot_count, frames * 128)]
    convert_element_type x12 -> x0, local copies, waits for them, and re-layouts: 9.67 us -> none  [push_per_offset(): jnp.dot(placing, gathered, preferred_element_type=jnp.float32)]
  transfers between devices with their start and end apart: 12 -> 0, of which waited for: 5 -> 0; matrix products, arithmetic and copies ran while one was open for 1% -> 0% of each run, Pallas kernels for 0% -> 0%
where the time goes in v1:
time: 35.9 us; the launch traced here: 35.7 us
  Pallas kernels  30.8 us (86%)
  local copies, waits for them, and re-layouts  4.88 us (14%)
    pallas_call x1, Pallas kernels, local(): pl.pallas_call(functools.partial(update_kernel, count, chunks), out_shape...  30.8 us
    unnamed x15, local copies, waits for them, and re-layouts  4.88 us

profile of v1, /device:TPU:0, one launch (start us, length us, event | category | flops | bytes accessed | tf_op | source)
XLA Modules:
  0.0 35.7 jit_solution(12890840007873518634)
XLA Ops:
  0.0 0.0 copy-start.5
  0.0 0.7 %copy.8.sensor_ref = s32[1,12,64]{2,1,0:T(8,128)S(1)} copy(s32[1,12,64]{2,0,1:T(1,128)} %param.11) | data formatting | bytes 6144 | tf_op args[4]
  0.7 0.0 copy-done.5
  0.7 0.0 copy-start.3
  0.7 0.0 copy-start.4
  0.7 0.6 %copy-done.3 = f32[8]{0:T(128)S(1)} copy-done((f32[8]{0:T(128)S(1)}, f32[8]{0:T(128)}, u32[]{:S(2)}) %copy-start.3) | copy-done | bytes 56
  1.4 0.0 copy-done.4
  1.4 0.0 copy-start
  1.4 1.0 %copy-done = bf16[12,128,128]{2,1,0:T(8,128)(2,1)S(1)} copy-done((bf16[12,128,128]{2,1,0:T(8,128)(2,1)S(1)}, bf16[12,128,128]{2,1,0:T(8,128)(2,1)}, u32[]{:S(2)}) %copy-start) | copy-done | bytes 393240
  2.4 0.0 copy-start.1
  2.4 0.9 %copy-done.1 = bf16[64,8,128]{2,1,0:T(8,128)(2,1)S(1)} copy-done((bf16[64,8,128]{2,1,0:T(8,128)(2,1)S(1)}, bf16[64,8,128]{2,1,0:T(8,128)(2,1)}, u32[]{:S(2)}) %copy-start.1) | copy-done | bytes 131096
  3.3 0.0 copy-start.2
  3.3 0.9 %copy-done.2 = bf16[64,8,128]{2,1,0:T(8,128)(2,1)S(1)} copy-done((bf16[64,8,128]{2,1,0:T(8,128)(2,1)S(1)}, bf16[64,8,128]{2,1,0:T(8,128)(2,1)}, u32[]{:S(2)}) %copy-start.2) | copy-done | bytes 131096
  4.2 30.8 %shard_map.73 = f32[512,128]{1,0:T(8,128)S(1)} custom-call(bf16[64,8,128]{2,1,0:T(8,128)(2,1)S(1)} %copy-done.1, bf16[64,8,128]{2,1,0:T(8,128)(2,1)S(1)} %copy-done.2, f32[1,8]{1,0:T(1,128)S(1)} %bitcast.3, bf16[12,128,128]{2,1,0:T(8,128)(2,1)S(1)} %copy-done, s32[1,12,64]{2,1,0:T(8,128)S(1)} %copy.8.sensor_ref, s32[1,12,64]{2,1,0:T(8,128)S(1)} %copy.9.voxel_ref, ...), custom_call_target="tpu_custom_call" | custom-call | tf_op jit(solution)/shard_map/pallas_call | solution.py:229
  35.0 0.7 %copy.11 = f32[64,8,128]{2,1,0:T(8,128)} copy(f32[64,8,128]{2,1,0:T(8,128)S(1)} %bitcast.2) | data formatting | bytes 524288
  (1 shorter events, 0.0 us)
Async XLA Ops:
  0.0 0.7 %copy-start.5 = (s32[1,12,64]{2,0,1:T(1,128)S(1)}, s32[1,12,64]{2,0,1:T(1,128)}, u32[]{:S(2)}) copy-start(s32[1,12,64]{2,0,1:T(1,128)} %param.12) | copy-start | bytes 9220
  0.7 0.7 %copy-start.3 = (f32[8]{0:T(128)S(1)}, f32[8]{0:T(128)}, u32[]{:S(2)}) copy-start(f32[8]{0:T(128)} %param.9) | copy-start | bytes 100
  0.7 0.7 %copy-start.4 = (s32[1,12]{1,0:T(1,128)S(1)}, s32[1,12]{1,0:T(1,128)}, u32[]{:S(2)}) copy-start(s32[1,12]{1,0:T(1,128)} %live_ref.1) | copy-start | bytes 148
  1.4 1.0 %copy-start = (bf16[12,128,128]{2,1,0:T(8,128)(2,1)S(1)}, bf16[12,128,128]{2,1,0:T(8,128)(2,1)}, u32[]{:S(2)}) copy-start(bf16[12,128,128]{2,1,0:T(8,128)(2,1)} %psf_ref.1) | copy-start | bytes 1179652
  2.4 0.9 %copy-start.1 = (bf16[64,8,128]{2,1,0:T(8,128)(2,1)S(1)}, bf16[64,8,128]{2,1,0:T(8,128)(2,1)}, u32[]{:S(2)}) copy-start(bf16[64,8,128]{2,1,0:T(8,128)(2,1)} %volume_ref.1) | copy-start | bytes 393220
  3.3 0.9 %copy-start.2 = (bf16[64,8,128]{2,1,0:T(8,128)(2,1)S(1)}, bf16[64,8,128]{2,1,0:T(8,128)(2,1)}, u32[]{:S(2)}) copy-start(bf16[64,8,128]{2,1,0:T(8,128)(2,1)} %measured_ref.1) | copy-start | bytes 393220

commit v2 on v1

v2 whole, which is shorter than its diff:
```python
import functools

import jax
import jax.numpy as jnp
from jax import lax
from jax.experimental import pallas as pl
from jax.experimental.pallas import tpu as pltpu
from jax.sharding import PartitionSpec as P

REACH = 3
PANELS = 2 * REACH + 2
FAR = -1000000.0
SHIFTS = (1, -1, 2, -2, 3, -3)
MESH = pl.DeviceIdType.MESH
OUT_KINDS = 7


def update_kernel(
    count,
    chunks,
    volume_hbm,
    measured_hbm,
    background_ref,
    psf_hbm,
    sensor_hbm,
    voxel_hbm,
    live_ref,
    out_ref,
    volume_ref,
    measured_ref,
    psf_ref,
    sensor_ref,
    voxel_ref,
    volume_win,
    ratio_win,
    voxel_win,
    volume_f32,
    measured_f32,
    place_fwd,
    place_bwd,
    psf_turned,
    ones_rows,
    norm,
    load_sem,
    send_list,
    recv_list,
    send_vol,
    recv_vol,
    send_ratio,
    recv_ratio,
):
    me = lax.axis_index("vox")
    core = lax.rem(me, 2)
    sibling = me + 1 - 2 * core
    blocks, frames, width = volume_ref.shape
    offsets = psf_ref.shape[0] // width
    per = frames // chunks
    lanes = per * width
    f32, bf16 = jnp.float32, jnp.bfloat16
    square = count == 8

    def inside(shift):
        return (me + shift >= 0) & (me + shift < count)

    loads = [
        pltpu.make_async_copy(source, target, load_sem.at[i])
        for i, (source, target) in enumerate(
            (
                (volume_hbm, volume_ref),
                (sensor_hbm, sensor_ref),
                (voxel_hbm, voxel_ref),
                (measured_hbm, measured_ref),
                (psf_hbm, psf_ref),
            )
        )
    ]
    for load in loads:
        load.start()

    barrier = pltpu.get_barrier_semaphore()
    for shift in SHIFTS:

        @pl.when(inside(shift))
        def _():
            pl.semaphore_signal(barrier, inc=1, device_id={"vox": me + shift}, device_id_type=MESH)

    peers = jnp.minimum(me, REACH) + jnp.minimum(count - 1 - me, REACH)
    if square:
        at_corner = (me == 0) | (me == 3) | (me == 4) | (me == 7)
        across = lax.rem(me + 4, 8)
        peers = peers + jnp.where(at_corner, 1, 0)

        @pl.when(at_corner)
        def _():
            pl.semaphore_signal(barrier, inc=1, device_id={"vox": across}, device_id_type=MESH)

    loads[0].wait()
    volume_f32[...] = volume_ref[...].astype(f32).reshape(blocks * frames, width)
    for frame in range(frames):
        rows = volume_f32[pl.ds(frame, blocks, stride=frames), :]
        j, k = divmod(frame, per)
        volume_win[j, REACH, :, k * width : (k + 1) * width] = rows.astype(bf16)

    pl.semaphore_wait(barrier, peers)

    class Panels:
        def __init__(self, win, send_sem, recv_sem):
            self.win, self.send_sem, self.recv_sem = win, send_sem, recv_sem

        def copy(self, j, kind, held, target):
            place = REACH + (me + held) - target
            return pltpu.make_async_remote_copy(
                src_ref=self.win.at[j, REACH + held],
                dst_ref=self.win.at[j, place],
                send_sem=self.send_sem.at[j, kind],
                recv_sem=self.recv_sem.at[j, place],
                device_id={"vox": target},
                device_id_type=MESH,
            )

        def wait_panel(self, j, place):
            pltpu.make_async_remote_copy(
                src_ref=self.win.at[j, REACH],
                dst_ref=self.win.at[j, REACH + place],
                send_sem=self.send_sem.at[j, 0],
                recv_sem=self.recv_sem.at[j, REACH + place],
                device_id={"vox": me},
                device_id_type=MESH,
            ).wait_recv()

        def own(self):
            far = me + 6 * core - 3
            direct_up, direct_down = inside(2), inside(-2)
            if square:
                direct_up = direct_up & (me != 2) & (me != 3)
                direct_down = direct_down & (me != 4) & (me != 5)
            return (
                (0, 0, far, (far >= 0) & (far < count)),
                (1, 0, me + 2, direct_up),
                (2, 0, me - 2, direct_down),
                (3, 0, sibling, me >= 0),
            )

        def passed(self):
            return ((4, 2, sibling, inside(2)), (5, -2, sibling, inside(-2)))

        def relays(self):
            if not square:
                return ()
            return (
                (6, 2, me + 4, me == 0),
                (6, -2, me - 4, me == 7),
                (6, 3, me + 1, me == 1),
                (6, -3, me - 1, me == 6),
            )

        def send_own(self, j):
            for kind, held, target, use in self.own():

                @pl.when(use)
                def _():
                    self.copy(j, kind, held, target).start()

        def pass_on(self, j):
            for shift in (2, -2):

                @pl.when(inside(shift))
                def _():
                    self.wait_panel(j, shift)

            far = 6 * core - 3

            @pl.when((me + far >= 0) & (me + far < count))
            def _():
                self.wait_panel(j, far)

            for kind, held, target, use in (*self.relays(), *self.passed()):

                @pl.when(use)
                def _():
                    self.copy(j, kind, held, target).start()

        def wait_rest(self, j):
            self.wait_panel(j, 1 - 2 * core)
            for shift in (2, -2):
                place = 1 - 2 * core + shift

                @pl.when((me + place >= 0) & (me + place < count))
                def _():
                    self.wait_panel(j, place)

        def wait_sent(self, j):
            for kind, held, target, use in (*self.own(), *self.relays(), *self.passed()):

                @pl.when(use)
                def _():
                    self.copy(j, kind, held, target).wait_send()

    volumes = Panels(volume_win, send_vol, recv_vol)
    ratios = Panels(ratio_win, send_ratio, recv_ratio)

    def list_copy(i):
        shift = SHIFTS[i]
        return pltpu.make_async_remote_copy(
            src_ref=voxel_win.at[REACH],
            dst_ref=voxel_win.at[REACH - shift],
            send_sem=send_list.at[i],
            recv_sem=recv_list.at[i],
            device_id={"vox": me + shift},
            device_id_type=MESH,
        )

    for j in range(chunks):
        volumes.send_own(j)

    loads[1].wait()
    loads[2].wait()
    sensor_iota = lax.broadcasted_iota(jnp.int32, (blocks, blocks), 0)
    slot_iota = lax.broadcasted_iota(jnp.int32, (1, blocks), 1)
    lane_iota = lax.broadcasted_iota(jnp.int32, (blocks, 128), 1)
    by_sensor = []
    table = jnp.full((blocks, 128), FAR, f32)
    for o in range(offsets):
        live = slot_iota < live_ref[0, o]
        sensor_row = jnp.where(live, sensor_ref[o], -1)
        voxel_row = voxel_ref[o].astype(f32) - FAR
        column = jnp.sum(
            jnp.where(sensor_row == sensor_iota, voxel_row, 0.0), axis=1, keepdims=True
        ) + FAR
        by_sensor.append(column)
        table = jnp.where(lane_iota == o, column, table)
    voxel_win[REACH, :, :blocks] = table.T[:16, :]
    voxel_win[REACH, :, blocks:] = jnp.full((16, 128 - blocks), FAR, f32)

    for i, shift in enumerate(SHIFTS):

        @pl.when(inside(shift))
        def _():
            list_copy(i).start()

    for j in range(chunks):
        volume_win[j, PANELS - 1] = jnp.zeros((blocks, lanes), bf16)
        ratio_win[j, PANELS - 1] = jnp.zeros((blocks, lanes), bf16)
    for shift in SHIFTS:

        @pl.when(jnp.logical_not(inside(shift)))
        def _():
            for j in range(chunks):
                volume_win[j, REACH + shift] = jnp.zeros((blocks, lanes), bf16)
                ratio_win[j, REACH + shift] = jnp.zeros((blocks, lanes), bf16)
            voxel_win[REACH + shift] = jnp.full((16, 128), FAR, f32)

    volumes.pass_on(0)

    base = ((me - REACH) * blocks).astype(f32)
    win_iota = lax.broadcasted_iota(jnp.int32, (1, PANELS * blocks), 1).astype(f32) + base
    for o in range(offsets):
        place_fwd[o * blocks : (o + 1) * blocks, :] = jnp.where(
            by_sensor[o] == win_iota, 1.0, 0.0
        ).astype(bf16)
    volumes.pass_on(1)

    loads[3].wait()
    measured_f32[...] = measured_ref[...].astype(f32).reshape(blocks * frames, width)
    loads[4].wait()

    def joined(placed):
        return jnp.concatenate(
            [
                jnp.concatenate(
                    [
                        placed[o * blocks : (o + 1) * blocks, k * width : (k + 1) * width]
                        for o in range(offsets)
                    ],
                    axis=1,
                )
                for k in range(per)
            ],
            axis=0,
        )

    def forward(j):
        volumes.wait_rest(j)
        window = volume_win[j].reshape(PANELS * blocks, lanes)
        placed = jnp.dot(place_fwd[...], window, preferred_element_type=f32).astype(bf16)
        projected = jnp.dot(joined(placed), psf_ref[...], preferred_element_type=f32)
        for k in range(per):
            frame = j * per + k
            recorded = measured_f32[pl.ds(frame, blocks, stride=frames), :]
            ratio = recorded / (projected[k * blocks : (k + 1) * blocks] + background_ref[0, frame])
            ratio_win[j, REACH, :, k * width : (k + 1) * width] = ratio.astype(bf16)
        ratios.send_own(j)

    def backward(j):
        ratios.wait_rest(j)
        window = ratio_win[j].reshape(PANELS * blocks, lanes)
        summed = jnp.dot(place_bwd[...], window, preferred_element_type=f32)
        high = summed.astype(bf16)
        low = (summed - high.astype(f32)).astype(bf16)
        back = jnp.dot(joined(high), psf_turned[...], preferred_element_type=f32)
        back = back + jnp.dot(joined(low), psf_turned[...], preferred_element_type=f32)
        for k in range(per):
            frame = j * per + k
            current = volume_f32[pl.ds(frame, blocks, stride=frames), :]
            out_ref[pl.ds(frame, blocks, stride=frames), :] = (
                current * back[k * blocks : (k + 1) * blocks] / norm[...]
            )

    forward(0)
    volumes.pass_on(2)
    forward(1)
    volumes.pass_on(3)
    ratios.pass_on(0)
    forward(2)
    ratios.pass_on(1)
    forward(3)
    ratios.pass_on(2)

    for i, shift in enumerate(SHIFTS):

        @pl.when(inside(-shift))
        def _():
            list_copy(i).wait_recv()

    for o in range(offsets):
        tile = slice(o * width, (o + 1) * width)
        psf_turned[tile, :] = psf_ref[tile, :].astype(f32).T.astype(bf16)
    tables = jnp.concatenate(
        [voxel_win[d, :, :blocks] for d in range(PANELS - 1)]
        + [jnp.full((16, blocks), FAR, f32)],
        axis=1,
    )
    voxel_iota = lax.broadcasted_iota(jnp.int32, (blocks, 1), 0).astype(f32) + (
        me * blocks
    ).astype(f32)
    for o in range(offsets):
        hits = jnp.where(tables[o : o + 1, :] == voxel_iota, 1.0, 0.0)
        place_bwd[o * blocks : (o + 1) * blocks, :] = hits.astype(bf16)
        pairs = jnp.sum(hits, axis=1, keepdims=True)
        ones_rows[:, o * width : (o + 1) * width] = jnp.broadcast_to(pairs, (blocks, width)).astype(
            bf16
        )
    norm[...] = jnp.dot(ones_rows[...], psf_turned[...], preferred_element_type=f32)

    ratios.pass_on(3)
    for j in range(chunks):
        backward(j)

    for i, shift in enumerate(SHIFTS):

        @pl.when(inside(shift))
        def _():
            list_copy(i).wait_send()

    for j in range(chunks):
        volumes.wait_sent(j)
        ratios.wait_sent(j)


def local(count, volume, measured, background, psf_tiles, pair_sensor, pair_voxel, pair_count):
    blocks, frames, width = volume.shape
    offsets = psf_tiles.shape[0]
    chunks = 4
    lanes = frames // chunks * width
    smem = pl.BlockSpec(memory_space=pltpu.SMEM)
    anywhere = pl.BlockSpec(memory_space=pl.ANY)
    links = len(SHIFTS)
    f32, bf16, dma = jnp.float32, jnp.bfloat16, pltpu.SemaphoreType.DMA
    updated = pl.pallas_call(
        functools.partial(update_kernel, count, chunks),
        out_shape=jax.ShapeDtypeStruct((blocks * frames, width), f32),
        in_specs=[anywhere, anywhere, smem, anywhere, anywhere, anywhere, smem],
        out_specs=pl.BlockSpec(memory_space=pltpu.VMEM),
        scratch_shapes=[
            pltpu.VMEM(volume.shape, bf16),
            pltpu.VMEM(measured.shape, bf16),
            pltpu.VMEM((offsets * width, width), bf16),
            pltpu.VMEM((offsets, 1, blocks), jnp.int32),
            pltpu.VMEM((offsets, 1, blocks), jnp.int32),
            pltpu.VMEM((chunks, PANELS, blocks, lanes), bf16),
            pltpu.VMEM((chunks, PANELS, blocks, lanes), bf16),
            pltpu.VMEM((PANELS - 1, 16, 128), f32),
            pltpu.VMEM((blocks * frames, width), f32),
            pltpu.VMEM((blocks * frames, width), f32),
            pltpu.VMEM((offsets * blocks, PANELS * blocks), bf16),
            pltpu.VMEM((offsets * blocks, PANELS * blocks), bf16),
            pltpu.VMEM((offsets * width, width), bf16),
            pltpu.VMEM((blocks, offsets * width), bf16),
            pltpu.VMEM((blocks, width), f32),
            dma((5,)),
            dma((links,)),
            dma((links,)),
            dma((chunks, OUT_KINDS)),
            dma((chunks, PANELS - 1)),
            dma((chunks, OUT_KINDS)),
            dma((chunks, PANELS - 1)),
        ],
        compiler_params=pltpu.CompilerParams(
            collective_id=0, has_side_effects=True, vmem_limit_bytes=56 * 1024 * 1024
        ),
    )(
        volume,
        measured,
        background.reshape(1, frames),
        psf_tiles.reshape(offsets * width, width),
        pair_sensor.reshape(offsets, 1, blocks),
        pair_voxel.reshape(offsets, 1, blocks),
        pair_count,
    )
    return updated.reshape(blocks, frames, width)


def solution(mesh):
    return jax.shard_map(
        functools.partial(local, mesh.shape["vox"]),
        mesh=mesh,
        in_specs=(
            P("vox", "frm", None),
            P("vox", "frm", None),
            P("frm"),
            P(),
            P("vox", None, None),
            P("vox", None, None),
            P("vox", None),
        ),
        out_specs=P("vox", "frm", None),
        check_vma=False,
    )
```

time: 35.9 us -> 30.9 us (0.86)
  the two profiles are of different devices: /device:TPU:0 before, /device:TPU:29 now
where the time goes in v2:
time: 30.9 us; the launch traced here: 30.7 us
  Pallas kernels  29.1 us (94%)
  local copies, waits for them, and re-layouts  1.67 us (5%)
    pallas_call x1, Pallas kernels, local(): pl.pallas_call(functools.partial(update_kernel, count, chunks), out_shape...  29.1 us
    unnamed x1, local copies, waits for them, and re-layouts  1.67 us

profile of v2, /device:TPU:29, one launch (start us, length us, event | category | flops | bytes accessed | tf_op | source)
XLA Modules:
  0.0 30.7 jit_solution(13838590709655885703)
XLA Ops:
  0.0 29.1 %shard_map.73 = f32[512,128]{1,0:T(8,128)} custom-call(bf16[64,8,128]{2,1,0:T(8,128)(2,1)} %volume_hbm.1, bf16[64,8,128]{2,1,0:T(8,128)(2,1)} %measured_hbm.1, f32[1,8]{1,0:T(1,128)} %bitcast.9, bf16[1536,128]{1,0:T(8,128)(2,1)} %bitcast.6, s32[12,1,64]{2,1,0:T(1,128)} %bitcast.7, s32[12,1,64]{2,1,0:T(1,128)} %bitcast.8, s32[1,12]{1,0:T(1,128)} %live_ref.1), custom_call_target="tpu_custom_call" | custom-call | tf_op jit(solution)/shard_map/pallas_call | solution.py:369
  29.1 1.7 %copy.9 = f32[64,8,128]{2,1,0:T(8,128)} copy(f32[64,8,128]{2,1,0:T(8,128)} %bitcast.5) | data formatting | bytes 524288

commit v3 on v2

--- a/solution.py
+++ b/solution.py
@@ -12,7 +12,7 @@
 FAR = -1000000.0
 SHIFTS = (1, -1, 2, -2, 3, -3)
 MESH = pl.DeviceIdType.MESH
-OUT_KINDS = 7
+OUT_KINDS = 6
 
 
 def update_kernel(
@@ -57,7 +57,6 @@
     per = frames // chunks
     lanes = per * width
     f32, bf16 = jnp.float32, jnp.bfloat16
-    square = count == 8
 
     def inside(shift):
         return (me + shift >= 0) & (me + shift < count)
@@ -85,14 +84,6 @@
             pl.semaphore_signal(barrier, inc=1, device_id={"vox": me + shift}, device_id_type=MESH)
 
     peers = jnp.minimum(me, REACH) + jnp.minimum(count - 1 - me, REACH)
-    if square:
-        at_corner = (me == 0) | (me == 3) | (me == 4) | (me == 7)
-        across = lax.rem(me + 4, 8)
-        peers = peers + jnp.where(at_corner, 1, 0)
-
-        @pl.when(at_corner)
-        def _():
-            pl.semaphore_signal(barrier, inc=1, device_id={"vox": across}, device_id_type=MESH)
 
     loads[0].wait()
     volume_f32[...] = volume_ref[...].astype(f32).reshape(blocks * frames, width)
@@ -131,9 +122,6 @@
         def own(self):
             far = me + 6 * core - 3
             direct_up, direct_down = inside(2), inside(-2)
-            if square:
-                direct_up = direct_up & (me != 2) & (me != 3)
-                direct_down = direct_down & (me != 4) & (me != 5)
             return (
                 (0, 0, far, (far >= 0) & (far < count)),
                 (1, 0, me + 2, direct_up),
@@ -144,16 +132,6 @@
         def passed(self):
             return ((4, 2, sibling, inside(2)), (5, -2, sibling, inside(-2)))
 
-        def relays(self):
-            if not square:
-                return ()
-            return (
-                (6, 2, me + 4, me == 0),
-                (6, -2, me - 4, me == 7),
-                (6, 3, me + 1, me == 1),
-                (6, -3, me - 1, me == 6),
-            )
-
         def send_own(self, j):
             for kind, held, target, use in self.own():
 
@@ -168,20 +146,20 @@
                 def _():
                     self.wait_panel(j, shift)
 
+            for kind, held, target, use in self.passed():
+
+                @pl.when(use)
+                def _():
+                    self.copy(j, kind, held, target).start()
+
+        def wait_rest(self, j):
+            self.wait_panel(j, 1 - 2 * core)
             far = 6 * core - 3
 
             @pl.when((me + far >= 0) & (me + far < count))
             def _():
                 self.wait_panel(j, far)
 
-            for kind, held, target, use in (*self.relays(), *self.passed()):
-
-                @pl.when(use)
-                def _():
-                    self.copy(j, kind, held, target).start()
-
-        def wait_rest(self, j):
-            self.wait_panel(j, 1 - 2 * core)
             for shift in (2, -2):
                 place = 1 - 2 * core + shift
 
@@ -190,7 +168,7 @@
                     self.wait_panel(j, place)
 
         def wait_sent(self, j):
-            for kind, held, target, use in (*self.own(), *self.relays(), *self.passed()):
+            for kind, held, target, use in (*self.own(), *self.passed()):
 
                 @pl.when(use)
                 def _():
@@ -210,8 +188,7 @@
             device_id_type=MESH,
         )
 
-    for j in range(chunks):
-        volumes.send_own(j)
+    volumes.send_own(0)
 
     loads[1].wait()
     loads[2].wait()
@@ -238,6 +215,9 @@
         def _():
             list_copy(i).start()
 
+    for j in range(1, chunks):
+        volumes.send_own(j)
+
     for j in range(chunks):
         volume_win[j, PANELS - 1] = jnp.zeros((blocks, lanes), bf16)
         ratio_win[j, PANELS - 1] = jnp.zeros((blocks, lanes), bf16)
@@ -249,20 +229,6 @@
                 volume_win[j, REACH + shift] = jnp.zeros((blocks, lanes), bf16)
                 ratio_win[j, REACH + shift] = jnp.zeros((blocks, lanes), bf16)
             voxel_win[REACH + shift] = jnp.full((16, 128), FAR, f32)
-
-    volumes.pass_on(0)
-
-    base = ((me - REACH) * blocks).astype(f32)
-    win_iota = lax.broadcasted_iota(jnp.int32, (1, PANELS * blocks), 1).astype(f32) + base
-    for o in range(offsets):
-        place_fwd[o * blocks : (o + 1) * blocks, :] = jnp.where(
-            by_sensor[o] == win_iota, 1.0, 0.0
-        ).astype(bf16)
-    volumes.pass_on(1)
-
-    loads[3].wait()
-    measured_f32[...] = measured_ref[...].astype(f32).reshape(blocks * frames, width)
-    loads[4].wait()
 
     def joined(placed):
         return jnp.concatenate(
@@ -306,25 +272,27 @@
                 current * back[k * blocks : (k + 1) * blocks] / norm[...]
             )
 
-    forward(0)
-    volumes.pass_on(2)
-    forward(1)
-    volumes.pass_on(3)
-    ratios.pass_on(0)
-    forward(2)
-    ratios.pass_on(1)
-    forward(3)
-    ratios.pass_on(2)
-
+    base = ((me - REACH) * blocks).astype(f32)
+    win_iota = lax.broadcasted_iota(jnp.int32, (1, PANELS * blocks), 1).astype(f32) + base
+    for o in range(offsets):
+        place_fwd[o * blocks : (o + 1) * blocks, :] = jnp.where(
+            by_sensor[o] == win_iota, 1.0, 0.0
+        ).astype(bf16)
+    loads[3].wait()
+    measured_f32[...] = measured_ref[...].astype(f32).reshape(blocks * frames, width)
+    loads[4].wait()
+
+    volumes.pass_on(0)
+    for o in range(offsets):
+        tile = slice(o * width, (o + 1) * width)
+        psf_turned[tile, :] = psf_ref[tile, :].astype(f32).T.astype(bf16)
+    volumes.pass_on(1)
     for i, shift in enumerate(SHIFTS):
 
         @pl.when(inside(-shift))
         def _():
             list_copy(i).wait_recv()
 
-    for o in range(offsets):
-        tile = slice(o * width, (o + 1) * width)
-        psf_turned[tile, :] = psf_ref[tile, :].astype(f32).T.astype(bf16)
     tables = jnp.concatenate(
         [voxel_win[d, :, :blocks] for d in range(PANELS - 1)]
         + [jnp.full((16, blocks), FAR, f32)],
@@ -342,9 +310,21 @@
         )
     norm[...] = jnp.dot(ones_rows[...], psf_turned[...], preferred_element_type=f32)
 
+
+    forward(0)
+    volumes.pass_on(2)
+    forward(1)
+    volumes.pass_on(3)
+    forward(2)
+    ratios.pass_on(0)
+    forward(3)
+    ratios.pass_on(1)
+    backward(0)
+    ratios.pass_on(2)
+    backward(1)
     ratios.pass_on(3)
-    for j in range(chunks):
-        backward(j)
+    backward(2)
+    backward(3)
 
     for i, shift in enumerate(SHIFTS):
 

time: 30.9 us -> 24.9 us (0.81)
  the two profiles are of different devices: /device:TPU:29 before, /device:TPU:0 now
where the time goes in v3:
time: 24.9 us; the launch traced here: 24.7 us
  Pallas kernels  23.1 us (93%)
  local copies, waits for them, and re-layouts  1.67 us (7%)
    pallas_call x1, Pallas kernels, local(): pl.pallas_call(functools.partial(update_kernel, count, chunks), out_shape...  23.1 us
    unnamed x1, local copies, waits for them, and re-layouts  1.67 us

profile of v3, /device:TPU:0, one launch (start us, length us, event | category | flops | bytes accessed | tf_op | source)
XLA Modules:
  0.0 24.7 jit_solution(13686901352658709078)
XLA Ops:
  0.0 23.1 %shard_map.73 = f32[512,128]{1,0:T(8,128)} custom-call(bf16[64,8,128]{2,1,0:T(8,128)(2,1)} %volume_hbm.1, bf16[64,8,128]{2,1,0:T(8,128)(2,1)} %measured_hbm.1, f32[1,8]{1,0:T(1,128)} %bitcast.9, bf16[1536,128]{1,0:T(8,128)(2,1)} %bitcast.6, s32[12,1,64]{2,1,0:T(1,128)} %bitcast.7, s32[12,1,64]{2,1,0:T(1,128)} %bitcast.8, s32[1,12]{1,0:T(1,128)} %live_ref.1), custom_call_target="tpu_custom_call" | custom-call | tf_op jit(solution)/shard_map/pallas_call | solution.py:349
  23.1 1.7 %copy.9 = f32[64,8,128]{2,1,0:T(8,128)} copy(f32[64,8,128]{2,1,0:T(8,128)} %bitcast.5) | data formatting | bytes 524288

commit v4 on v3

--- a/solution.py
+++ b/solution.py
@@ -123,9 +123,9 @@
             far = me + 6 * core - 3
             direct_up, direct_down = inside(2), inside(-2)
             return (
-                (0, 0, far, (far >= 0) & (far < count)),
                 (1, 0, me + 2, direct_up),
                 (2, 0, me - 2, direct_down),
+                (0, 0, far, (far >= 0) & (far < count)),
                 (3, 0, sibling, me >= 0),
             )
 
@@ -140,16 +140,11 @@
                     self.copy(j, kind, held, target).start()
 
         def pass_on(self, j):
-            for shift in (2, -2):
-
-                @pl.when(inside(shift))
-                def _():
-                    self.wait_panel(j, shift)
-
             for kind, held, target, use in self.passed():
 
                 @pl.when(use)
                 def _():
+                    self.wait_panel(j, held)
                     self.copy(j, kind, held, target).start()
 
         def wait_rest(self, j):
@@ -206,8 +201,9 @@
         ) + FAR
         by_sensor.append(column)
         table = jnp.where(lane_iota == o, column, table)
-    voxel_win[REACH, :, :blocks] = table.T[:16, :]
-    voxel_win[REACH, :, blocks:] = jnp.full((16, 128 - blocks), FAR, f32)
+    turned = table.T
+    voxel_win[REACH, :, :blocks] = turned[:8, :]
+    voxel_win[REACH, :, blocks:] = turned[8:16, :]
 
     for i, shift in enumerate(SHIFTS):
 
@@ -228,7 +224,7 @@
             for j in range(chunks):
                 volume_win[j, REACH + shift] = jnp.zeros((blocks, lanes), bf16)
                 ratio_win[j, REACH + shift] = jnp.zeros((blocks, lanes), bf16)
-            voxel_win[REACH + shift] = jnp.full((16, 128), FAR, f32)
+            voxel_win[REACH + shift] = jnp.full((8, 128), FAR, f32)
 
     def joined(placed):
         return jnp.concatenate(
@@ -287,22 +283,27 @@
         tile = slice(o * width, (o + 1) * width)
         psf_turned[tile, :] = psf_ref[tile, :].astype(f32).T.astype(bf16)
     volumes.pass_on(1)
+    forward(0)
+    volumes.pass_on(2)
     for i, shift in enumerate(SHIFTS):
 
         @pl.when(inside(-shift))
         def _():
             list_copy(i).wait_recv()
 
-    tables = jnp.concatenate(
-        [voxel_win[d, :, :blocks] for d in range(PANELS - 1)]
-        + [jnp.full((16, blocks), FAR, f32)],
-        axis=1,
-    )
+    tables = [
+        jnp.concatenate(
+            [voxel_win[d, :, side * blocks : (side + 1) * blocks] for d in range(PANELS - 1)]
+            + [jnp.full((8, blocks), FAR, f32)],
+            axis=1,
+        )
+        for side in range(2)
+    ]
     voxel_iota = lax.broadcasted_iota(jnp.int32, (blocks, 1), 0).astype(f32) + (
         me * blocks
     ).astype(f32)
     for o in range(offsets):
-        hits = jnp.where(tables[o : o + 1, :] == voxel_iota, 1.0, 0.0)
+        hits = jnp.where(tables[o // 8][o % 8 : o % 8 + 1, :] == voxel_iota, 1.0, 0.0)
         place_bwd[o * blocks : (o + 1) * blocks, :] = hits.astype(bf16)
         pairs = jnp.sum(hits, axis=1, keepdims=True)
         ones_rows[:, o * width : (o + 1) * width] = jnp.broadcast_to(pairs, (blocks, width)).astype(
@@ -311,8 +312,6 @@
     norm[...] = jnp.dot(ones_rows[...], psf_turned[...], preferred_element_type=f32)
 
 
-    forward(0)
-    volumes.pass_on(2)
     forward(1)
     volumes.pass_on(3)
     forward(2)
@@ -359,7 +358,7 @@
             pltpu.VMEM((offsets, 1, blocks), jnp.int32),
             pltpu.VMEM((chunks, PANELS, blocks, lanes), bf16),
             pltpu.VMEM((chunks, PANELS, blocks, lanes), bf16),
-            pltpu.VMEM((PANELS - 1, 16, 128), f32),
+            pltpu.VMEM((PANELS - 1, 8, 128), f32),
             pltpu.VMEM((blocks * frames, width), f32),
             pltpu.VMEM((blocks * frames, width), f32),
             pltpu.VMEM((offsets * blocks, PANELS * blocks), bf16),

time: 24.9 us -> 24.6 us (0.988)
  Pallas kernels: 23.1 us -> 22.8 us
    pallas_call x1, Pallas kernels: 23.1 us -> 22.8 us  [local(): pl.pallas_call(functools.partial(update_kernel, count, chunks), out_shape...]
where the time goes in v4:
time: 24.6 us; the launch traced here: 24.4 us
  Pallas kernels  22.8 us (93%)
  local copies, waits for them, and re-layouts  1.67 us (7%)
    pallas_call x1, Pallas kernels, local(): pl.pallas_call(functools.partial(update_kernel, count, chunks), out_shape...  22.8 us
    unnamed x1, local copies, waits for them, and re-layouts  1.67 us

profile of v4, /device:TPU:0, one launch (start us, length us, event | category | flops | bytes accessed | tf_op | source)
XLA Modules:
  0.0 24.4 jit_solution(6911865265753065850)
XLA Ops:
  0.0 22.8 %shard_map.73 = f32[512,128]{1,0:T(8,128)} custom-call(bf16[64,8,128]{2,1,0:T(8,128)(2,1)} %volume_hbm.1, bf16[64,8,128]{2,1,0:T(8,128)(2,1)} %measured_hbm.1, f32[1,8]{1,0:T(1,128)} %bitcast.9, bf16[1536,128]{1,0:T(8,128)(2,1)} %bitcast.6, s32[12,1,64]{2,1,0:T(1,128)} %bitcast.7, s32[12,1,64]{2,1,0:T(1,128)} %bitcast.8, s32[1,12]{1,0:T(1,128)} %live_ref.1), custom_call_target="tpu_custom_call" | custom-call | tf_op jit(solution)/shard_map/pallas_call | solution.py:348
  22.8 1.7 %copy.9 = f32[64,8,128]{2,1,0:T(8,128)} copy(f32[64,8,128]{2,1,0:T(8,128)} %bitcast.5) | data formatting | bytes 524288
